TPU v7x, 32 devices: a whole 2x2x4 slice. The times are simulated.
32 devices in a mesh: groups: 2 (over y), gx: 4 (over x, core), gy: 4 (over z).
Axes of the slice: x: 2, y: 2, z: 4, core: 2. Of those that a mesh axis runs over, the one named last changes fastest.
Arguments:
- activations: bfloat16 [128, 18432], P(('groups', 'gy'), 'gx'), parts along dimension 0, may hold values from -6 to 6
- query_weight: bfloat16 [18432, 6144], P('gx', 'gy'), may hold values from -0.046875 to 0.046875
- kv_weight: bfloat16 [18432, 512], P('gx', 'gy'), may hold values from -0.046875 to 0.046875
- ffn_weight: bfloat16 [18432, 36864], P('gx', 'gy'), may hold values from -0.046875 to 0.046875
- cache_keys: bfloat16 [128, 512, 256], P(('groups', 'gx', 'gy')), parts along dimension 0, may hold values from -520 to 520
- cache_values: bfloat16 [128, 512, 256], P(('groups', 'gx', 'gy')), parts along dimension 0, may hold values from -6 to 6
- cache_lengths: int32 [128], P(('groups', 'gx', 'gy')), parts along dimension 0, may hold values from 1 to 512, as said below
- slot_rows: int32 [128], P('groups'), parts along dimension 0, may hold values from 0 to 63, each once
Outputs:
- attended: bfloat16 [128, 6144], P(('groups', 'gx', 'gy')), parts along dimension 0
- ffn_hidden: bfloat16 [128, 36864], P(('groups', 'gx'), 'gy'), parts along dimension 0
There are 2 independent parts, one for each index of `groups`. A program takes and returns all parts, laid end to end along the dimension named above; an argument that names none is the same for every part. Nothing has to cross between parts.
Inputs may be any that keep to these rules, and one draw needn't show every extreme that they name: `cache_lengths`: each filled length is at least 1, and some slot is full in every draw.
All inputs are finite; a program needn't handle non-finite values.
Results may differ from a plain program's by a relative error of at most 0.012.
The roundings to bfloat16 on the way count: a program that leaves them out, or rounds other values in their place, can miss the bound.
Values may be sent and summed in bfloat16 or wider, within the bound.
A program may use at most 256 MiB of HBM per device.

v0:
```python
import jax
import jax.numpy as jnp
from jax import lax
from jax.sharding import PartitionSpec as P

DH = 256


def attend(query_heads, new_keys, new_values, cache_keys, cache_values, cache_lengths):
    scaling = float(query_heads.shape[-1]) ** (-0.5)
    scores = (
        jnp.einsum("rhd,rcd->rhc", query_heads, cache_keys, preferred_element_type=jnp.float32)
        * scaling
    )
    new_score = (
        jnp.einsum("rhd,rd->rh", query_heads, new_keys, preferred_element_type=jnp.float32)
        * scaling
    )
    positions = lax.broadcasted_iota(jnp.int32, (1, 1, cache_keys.shape[1]), 2)
    usable = positions < cache_lengths[:, None, None]
    scores = jnp.where(usable, scores, -jnp.inf)
    peak = jnp.maximum(jnp.max(scores, axis=-1), new_score)
    weights = jnp.exp(scores - peak[..., None])
    weight_new = jnp.exp(new_score - peak)
    totals = jnp.sum(weights, axis=-1) + weight_new
    probs = (weights / totals[..., None]).astype(jnp.bfloat16)
    prob_new = (weight_new / totals).astype(jnp.bfloat16)
    result = jnp.einsum("rhc,rcd->rhd", probs, cache_values, preferred_element_type=jnp.float32)
    result = (
        result
        + prob_new.astype(jnp.float32)[..., None] * new_values.astype(jnp.float32)[:, None, :]
    )
    return result.astype(jnp.bfloat16).reshape(query_heads.shape[0], -1)


def shards(
    activations,
    query_weight,
    kv_weight,
    ffn_weight,
    cache_keys,
    cache_values,
    cache_lengths,
    slot_rows,
):
    gx_count = lax.axis_size("gx")
    gy_count = lax.axis_size("gy")
    all_rows = lax.all_gather(activations, "gy", axis=0, tiled=True)
    batch_rows = all_rows.shape[0]
    per_device = batch_rows // (gx_count * gy_count)
    picked = jnp.take(all_rows, slot_rows, axis=0)
    query_part = jnp.dot(picked, query_weight, preferred_element_type=jnp.float32)
    pair_part = jnp.dot(picked, kv_weight, preferred_element_type=jnp.float32)
    query_sum, pair_sum = (
        lax.psum_scatter(query_part, "gx", scatter_dimension=0, tiled=True),
        lax.psum_scatter(pair_part, "gx", scatter_dimension=0, tiled=True),
    )
    query_own, pair_own = (
        lax.all_to_all(
            query_sum.astype(jnp.bfloat16), "gy", split_axis=0, concat_axis=1, tiled=True
        ),
        lax.all_to_all(
            pair_sum.astype(jnp.bfloat16), "gy", split_axis=0, concat_axis=1, tiled=True
        ),
    )
    head_count = query_own.shape[1] // DH
    query_heads = query_own.reshape(per_device, head_count, DH)
    attended = attend(
        query_heads, pair_own[:, :DH], pair_own[:, DH:], cache_keys, cache_values, cache_lengths
    )
    hidden_part = jnp.dot(all_rows, ffn_weight, preferred_element_type=jnp.float32)
    hidden_sum = lax.psum_scatter(hidden_part, "gx", scatter_dimension=1, tiled=True)
    activated = jax.nn.silu(hidden_sum).astype(jnp.bfloat16)
    ffn_hidden = lax.all_to_all(activated, "gx", split_axis=0, concat_axis=1, tiled=True)
    return (attended, ffn_hidden)


def solution(mesh):
    in_specs = (
        P(("groups", "gy"), "gx"),
        P("gx", "gy"),
        P("gx", "gy"),
        P("gx", "gy"),
        P(("groups", "gx", "gy"), None, None),
        P(("groups", "gx", "gy"), None, None),
        P(("groups", "gx", "gy")),
        P("groups"),
    )
    out_specs = (P(("groups", "gx", "gy"), None), P(("groups", "gx"), "gy"))
    return jax.shard_map(shards, mesh=mesh, in_specs=in_specs, out_specs=out_specs, check_vma=False)
```

profile of v0, /device:TPU:0, one launch (start us, length us, event | category | flops | bytes accessed | tf_op | source)
XLA Modules:
  0.0 128.3 jit_solution(802159407772531894)
XLA Ops:
  7.2 0.0 reduce-scatter.6.cloned.1.call-start
  7.2 0.8 compare_and_fusion
  8.0 0.7 compare_select_fusion
  8.6 18.4 %all_gather.3 = bf16[64,4608]{1,0:T(8,128)(2,1)S(1)} all-gather(bf16[16,4608]{1,0:T(8,128)(2,1)} %param.8), channel_id=1, replica_groups=mesh['groups'=2,'gx'=4,'gy'=4] {'gy'}, dimensions={0}, use_global_device_ids=true | all-gather | bytes 737280 | tf_op jit(solution)/shard_map/all_gather | solution.py:48
  27.0 0.9 gather_fusion
  27.9 1.0 fusion.3
  28.9 0.0 reduce-scatter.6.cloned.1.call-update
  29.0 0.0 reduce-scatter.4.cloned.1.call-start
  29.0 8.4 %fusion.4 = f32[64,1536]{1,0:T(8,128)} fusion(bf16[4608,1536]{1,0:T(8,128)(2,1)} %param.9, bf16[64,4608]{1,0:T(8,128)(2,1)S(1)} %gather_fusion, pred[64]{0:T(512)(128)(4,1)S(1)} %compare_and_fusion), kind=kOutput, calls=%fused_computation.9 | convolution fusion | flops 906264576 | bytes 15138880 | tf_op jit(solution)/shard_map/dot_general | solution.py:52
  37.4 0.0 reduce-scatter.4.cloned.1.call-update
  37.5 0.0 reduce-scatter.8.cloned.1.call-start
  37.5 31.1 %fusion.15 = f32[64,9216]{1,0:T(8,128)} fusion(bf16[64,4608]{1,0:T(8,128)(2,1)S(1)} %all_gather.3, bf16[4608,9216]{1,0:T(8,128)(2,1)} %param.11), kind=kOutput, calls=%fused_computation.31 | convolution fusion | flops 5435817984 | bytes 87883776 | tf_op jit(solution)/shard_map/dot_general | solution.py:71
  68.7 0.0 reduce-scatter.8.cloned.1.call-update
  68.7 0.0 reduce-scatter.6.cloned.1.call-done
  68.7 1.3 %convert_element_type.25 = bf16[16,128]{1,0:T(8,128)(2,1)} convert(f32[16,128]{1,0:T(8,128)} %reduce-scatter.6.cloned.1.call-done) | non-fusion elementwise | flops 2048 | bytes 12288 | tf_op jit(solution)/shard_map/convert_element_type | solution.py:63
  70.0 5.0 %all-to-all-start.1 = ((bf16[4,4,128]{2,1,0:T(4,128)(2,1)}), bf16[4,4,128]{2,1,0:T(4,128)(2,1)S(1)}, u32[]{:S(2)}, u32[]{:S(2)}) async-start(bf16[4,4,128]{2,1,0:T(4,128)(2,1)} %bitcast.1), calls=%async_computation.3 | async-start | bytes 8192 | tf_op jit(solution)/shard_map/all_to_all | solution.py:62
  75.0 0.1 iota_compare_fusion
  75.1 0.9 convert_element_type.24
  76.0 0.6 all_to_all.40
  76.6 4.0 %all-to-all-done.1 = bf16[4,4,128]{2,1,0:T(4,128)(2,1)S(1)} async-done(((bf16[4,4,128]{2,1,0:T(4,128)(2,1)}), bf16[4,4,128]{2,1,0:T(4,128)(2,1)S(1)}, u32[]{:S(2)}, u32[]{:S(2)}) %all-to-all-start.1) | async-done | bytes 4128 | tf_op jit(solution)/shard_map/all_to_all | solution.py:62
  80.6 3.3 %all-to-all-start = ((bf16[4,4,1536]{2,1,0:T(4,128)(2,1)}), bf16[4,4,1536]{2,1,0:T(4,128)(2,1)S(1)}, u32[]{:S(2)}, u32[]{:S(2)}) async-start(bf16[4,4,1536]{2,1,0:T(4,128)(2,1)} %all_to_all.40), calls=%async_computation.1 | async-start | bytes 98304 | tf_op jit(solution)/shard_map/all_to_all | solution.py:59
  83.9 5.7 %all-to-all-done = bf16[4,4,1536]{2,1,0:T(4,128)(2,1)S(1)} async-done(((bf16[4,4,1536]{2,1,0:T(4,128)(2,1)}), bf16[4,4,1536]{2,1,0:T(4,128)(2,1)S(1)}, u32[]{:S(2)}, u32[]{:S(2)}) %all-to-all-start) | async-done | bytes 49184 | tf_op jit(solution)/shard_map/all_to_all | solution.py:59
  89.6 0.1 fusion.8
  89.7 0.5 fusion.14
  90.2 0.2 fusion.5
  90.4 18.9 %reduce-scatter.8.cloned.1.call-done = f32[64,2304]{1,0:T(8,128)} async-done(((f32[64,9216]{1,0:T(8,128)}), f32[64,2304]{1,0:T(8,128)}) %reduce-scatter.8.cloned.1.call-update) | async-done | bytes 589840 | tf_op jit(solution)/shard_map/reduce_scatter | solution.py:72
  109.3 1.9 %multiply_convert_fusion = bf16[64,2304]{1,0:T(8,128)(2,1)} fusion(f32[64,2304]{1,0:T(8,128)} %reduce-scatter.8.cloned.1.call-done), kind=kLoop, calls=%fused_computation.6 | loop fusion | flops 737280 | bytes 884736 | tf_op jit(solution)/shard_map/convert_element_type | solution.py:73
  111.2 3.5 %all-to-all-start.2 = ((bf16[4,16,2304]{2,1,0:T(8,128)(2,1)}), bf16[4,16,2304]{2,1,0:T(8,128)(2,1)S(1)}, u32[]{:S(2)}, u32[]{:S(2)}) async-start(bf16[4,16,2304]{2,1,0:T(8,128)(2,1)} %bitcast.8), calls=%async_computation.5 | async-start | bytes 589824 | tf_op jit(solution)/shard_map/all_to_all | solution.py:74
  114.7 1.5 %fusion.2 = bf16[1,4,24,256]{3,2,1,0:T(8,128)(2,1)S(1)} fusion(bf16[4,512,256]{2,1,0:T(8,128)(2,1)} %param.13, f32[4,24,512]{2,1,0:T(8,128)S(1)} %get-tuple-element.7, f32[4,24]{1,0:T(4,128)S(1)} %get-tuple-element.3, f32[4,24]{1,0:T(4,128)S(1)} %multiply_maximum_fusion, f32[4,256]{1,0:T(4,128)S(1)} %get-tuple-element.4, f32[4,24]{1,0:T(4,128)S(1)} %get-tuple-element.2), kind=kOutput, calls=%fused_computation.5 | convolution fusion | flops 25387008 | bytes 1299584 | tf_op jit(solution)/shard_map/rhc,rcd->rhd/dot_general | solution.py:28
  116.2 0.6 copy.15
  116.9 4.2 %all-to-all-done.2 = bf16[4,16,2304]{2,1,0:T(8,128)(2,1)S(1)} async-done(((bf16[4,16,2304]{2,1,0:T(8,128)(2,1)}), bf16[4,16,2304]{2,1,0:T(8,128)(2,1)S(1)}, u32[]{:S(2)}, u32[]{:S(2)}) %all-to-all-start.2) | async-done | bytes 294944 | tf_op jit(solution)/shard_map/all_to_all | solution.py:74
  121.0 0.7 copy.14
  (13 shorter events, 0.1 us)
Async XLA Ops:
  7.2 20.8 %copy-start = (bf16[4608,128]{1,0:T(8,128)(2,1)S(1)}, bf16[4608,128]{1,0:T(8,128)(2,1)}, u32[]{:S(2)}) copy-start(bf16[4608,128]{1,0:T(8,128)(2,1)} %param.10) | copy-start | bytes 3538948
  7.2 61.5 %reduce-scatter.6.cloned.1.call-start = ((), (), s32[]{:S(2)}) async-start(), calls=%async_computation.7 | async-start | bytes 40960 | tf_op jit(solution)/shard_map/reduce_scatter | solution.py:56
  29.0 46.1 %reduce-scatter.4.cloned.1.call-start = ((), (), s32[]{:S(2)}) async-start(), calls=%async_computation.6 | async-start | bytes 491520 | tf_op jit(solution)/shard_map/reduce_scatter | solution.py:55
  37.4 37.5 %copy-start.2 = (s32[4]{0:T(128)S(1)}, s32[4]{0:T(128)}, u32[]{:S(2)}) copy-start(s32[4]{0:T(128)} %param.14) | copy-start | bytes 52
  37.4 52.3 %copy-start.1 = (bf16[4,512,256]{2,1,0:T(8,128)(2,1)S(1)}, bf16[4,512,256]{2,1,0:T(8,128)(2,1)}, u32[]{:S(2)}) copy-start(bf16[4,512,256]{2,1,0:T(8,128)(2,1)} %param.12) | copy-start | bytes 3145732
  37.5 71.8 %reduce-scatter.8.cloned.1.call-start = ((), (), s32[]{:S(2)}) async-start(), calls=%async_computation.8 | async-start | bytes 2949120 | tf_op jit(solution)/shard_map/reduce_scatter | solution.py:72
  70.0 10.5 %all-to-all-start.1 = ((bf16[4,4,128]{2,1,0:T(4,128)(2,1)}), bf16[4,4,128]{2,1,0:T(4,128)(2,1)S(1)}, u32[]{:S(2)}, u32[]{:S(2)}) async-start(bf16[4,4,128]{2,1,0:T(4,128)(2,1)} %bitcast.1), calls=%async_computation.3 | async-start | bytes 8192 | tf_op jit(solution)/shard_map/all_to_all | solution.py:62
  80.6 9.0 %all-to-all-start = ((bf16[4,4,1536]{2,1,0:T(4,128)(2,1)}), bf16[4,4,1536]{2,1,0:T(4,128)(2,1)S(1)}, u32[]{:S(2)}, u32[]{:S(2)}) async-start(bf16[4,4,1536]{2,1,0:T(4,128)(2,1)} %all_to_all.40), calls=%async_computation.1 | async-start | bytes 98304 | tf_op jit(solution)/shard_map/all_to_all | solution.py:59
  111.2 9.8 %all-to-all-start.2 = ((bf16[4,16,2304]{2,1,0:T(8,128)(2,1)}), bf16[4,16,2304]{2,1,0:T(8,128)(2,1)S(1)}, u32[]{:S(2)}, u32[]{:S(2)}) async-start(bf16[4,16,2304]{2,1,0:T(8,128)(2,1)} %bitcast.8), calls=%async_computation.5 | async-start | bytes 589824 | tf_op jit(solution)/shard_map/all_to_all | solution.py:74
Sparse Core Ops, SparseCore 0:
  29.1 20.7 reduce-scatter.5
  52.6 20.8 reduce-scatter.3
  76.2 33.0 reduce-scatter.7
where the time goes:
time: 129 us; the launch traced here: 128 us
  matrix products  42.7 us (33%)
  waiting for transfers between devices  32.7 us (25%)
  blocking collectives  18.4 us (14%)
  between operations  13.8 us (11%)
  starting transfers between devices  11.8 us (9%)
  other arithmetic  5.84 us (5%)
  local copies, waits for them, and re-layouts  3 us (2%)
    dot_general x1, matrix products, shards(): jnp.dot(all_rows, ffn_weight, preferred_element_type=jnp.float32)  31.1 us
    reduce_scatter x1, waiting for transfers between devices, shards(): lax.psum_scatter(hidden_part, 'gx', scatter_dimension=1, tiled=True)  18.9 us
    all_gather x1, blocking collectives, shards(): all_rows = lax.all_gather(activations, 'gy', axis=0, tiled=True)  18.4 us
    dot_general x1, matrix products, shards(): jnp.dot(picked, query_weight, preferred_element_type=jnp.float32)  8.39 us
    all_to_all x1, waiting for transfers between devices, shards(): lax.all_to_all(query_sum.astype(jnp.bfloat16), 'gy', split_axis=0, concat...  5.65 us
    all_to_all x1, starting transfers between devices, shards(): lax.all_to_all(pair_sum.astype(jnp.bfloat16), 'gy', split_axis=0, concat_...  4.97 us
    all_to_all x1, waiting for transfers between devices, shards(): lax.all_to_all(activated, 'gx', split_axis=0, concat_axis=1, tiled=True)  4.15 us
    all_to_all x1, waiting for transfers between devices, shards(): lax.all_to_all(pair_sum.astype(jnp.bfloat16), 'gy', split_axis=0, concat_...  3.96 us
  transfers between devices with their start and end apart: 6, of which 4 were waited for; matrix products, arithmetic and copies ran while one was open for 35% of the time, Pallas kernels for 0%

commit v1 on v0

--- a/solution.py
+++ b/solution.py
@@ -1,7 +1,13 @@
 import jax
 import jax.numpy as jnp
 from jax import lax
+from jax.experimental import pallas as pl
+from jax.experimental.pallas import tpu as pltpu
 from jax.sharding import PartitionSpec as P
+
+TILE = 512
+SLOTS = 10
+LAG = 3
 
 DH = 256
 
@@ -75,7 +81,244 @@
     return (attended, ffn_hidden)
 
 
+def send(src, dst, send_sem, recv_sem, axis, peer):
+    return pltpu.make_async_remote_copy(
+        src_ref=src,
+        dst_ref=dst,
+        send_sem=send_sem,
+        recv_sem=recv_sem,
+        device_id={axis: peer},
+        device_id_type=pl.DeviceIdType.MESH,
+    )
+
+
+def project_kernel(
+    act, perm, wq, wkv, wf,
+    hidden_out, pairs_out,
+    wbuf, kvbuf, rows, picked, part, own, fsend, frecv, qown, qsend, qrecv, pair_own, gathered,
+    wsem, kvsem, a_send, a_recv, f_send, f_recv, q_send, q_recv, g_send, g_recv,
+):
+    gx, gy = lax.axis_index("gx"), lax.axis_index("gy")
+    q_tiles = wq.shape[1] // TILE
+    f_tiles = wf.shape[1] // TILE
+    q_width = wq.shape[1]
+    ahead = SLOTS - q_tiles
+    block = act.shape[0]
+
+    def load_q(i):
+        return pltpu.make_async_copy(wq.at[:, pl.ds(i * TILE, TILE)], wbuf.at[i], wsem.at[i])
+
+    def load_f(t):
+        slot = lax.rem(t + q_tiles, SLOTS)
+        columns = pl.ds(pl.multiple_of(t * TILE, TILE), TILE)
+        return pltpu.make_async_copy(wf.at[:, columns], wbuf.at[slot], wsem.at[slot])
+
+    load_kv = pltpu.make_async_copy(wkv, kvbuf, kvsem)
+
+    for i in range(q_tiles):
+        load_q(i).start()
+    load_kv.start()
+
+    barrier = pltpu.get_barrier_semaphore()
+    for k in range(1, 4):
+        for axis, me in (("gx", gx), ("gy", gy)):
+            pl.semaphore_signal(
+                barrier, inc=1, device_id={axis: lax.rem(me + k, 4)},
+                device_id_type=pl.DeviceIdType.MESH,
+            )
+    pl.semaphore_wait(barrier, 6)
+
+    own_rows = pl.ds(pl.multiple_of(gy * block, block), block)
+    row_copies = []
+    for k in (2, 1, 3):
+        copy = send(
+            act, rows.at[own_rows], a_send.at[k - 1], a_recv.at[k - 1], "gy", lax.rem(gy + k, 4)
+        )
+        copy.start()
+        row_copies.append(copy)
+    for t in range(ahead):
+        load_f(jnp.int32(t)).start()
+    rows[own_rows, :] = act[...]
+    for copy in row_copies:
+        copy.wait()
+
+    picked[...] = jnp.dot(perm[...], rows[...], preferred_element_type=jnp.float32).astype(
+        jnp.bfloat16
+    )
+
+    def peer_rows(k):
+        return pl.ds(pl.multiple_of(lax.rem(gx + k, 4) * block, block), block)
+
+    for i in range(q_tiles + 1):
+        if i < q_tiles:
+            load_q(i).wait()
+            columns = slice(i * TILE, (i + 1) * TILE)
+            part[...] = jnp.dot(picked[...], wbuf[i], preferred_element_type=jnp.float32)
+            load_f(jnp.int32(ahead + i)).start()
+            width = TILE
+        else:
+            load_kv.wait()
+            width = kvbuf.shape[1]
+            columns = slice(q_width, q_width + width)
+            part[:, :width] = jnp.dot(
+                picked[...], kvbuf[...], preferred_element_type=jnp.float32
+            )
+        qown[:, columns] = part[peer_rows(0), :width]
+        for k in range(1, 4):
+            qsend[k - 1, :, columns] = part[peer_rows(k), :width]
+    q_copies = []
+    for k in (2, 1, 3):
+        copy = send(
+            qsend.at[k - 1], qrecv.at[k - 1], q_send.at[k - 1], q_recv.at[k - 1],
+            "gx", lax.rem(gx + k, 4),
+        )
+        copy.start()
+        q_copies.append(copy)
+
+    def f_copy(t, k):
+        return send(
+            fsend.at[t, k - 1], frecv.at[t, k - 1], f_send.at[t, k - 1], f_recv.at[t, k - 1],
+            "gx", lax.rem(gx + k, 4),
+        )
+
+    def multiply(t):
+        load_f(t).wait()
+        slot = lax.rem(t + q_tiles, SLOTS)
+        part[...] = jnp.dot(rows[...], wbuf[slot], preferred_element_type=jnp.float32)
+
+        @pl.when(t + SLOTS < f_tiles)
+        def _():
+            load_f(t + SLOTS).start()
+
+        for k in range(1, 4):
+            fsend[t, k - 1] = part[peer_rows(k), :].astype(jnp.bfloat16)
+            f_copy(t, k).start()
+        own[t] = part[peer_rows(0), :]
+
+    def finish(t):
+        total = own[t]
+        for k in range(1, 4):
+            f_copy(t, k).wait()
+            total = total + frecv[t, k - 1].astype(jnp.float32)
+        columns = pl.ds(pl.multiple_of(t * TILE, TILE), TILE)
+        hidden_out[:, columns] = (total / (1.0 + jnp.exp(-total))).astype(jnp.bfloat16)
+
+    def first(t, carry):
+        multiply(t)
+        return carry
+
+    def middle(t, carry):
+        multiply(t)
+        finish(t - LAG)
+        return carry
+
+    def last(t, carry):
+        finish(t)
+        return carry
+
+    lax.fori_loop(0, LAG, first, 0)
+
+    for copy in q_copies:
+        copy.wait()
+    pair_own[...] = (qown[...] + qrecv[0] + qrecv[1] + qrecv[2]).astype(jnp.bfloat16)
+    gathered[gy] = pair_own[...]
+    g_copies = []
+    for k in (2, 1, 3):
+        copy = send(
+            pair_own, gathered.at[gy], g_send.at[k - 1], g_recv.at[k - 1],
+            "gy", lax.rem(gy + k, 4),
+        )
+        copy.start()
+        g_copies.append(copy)
+
+    lax.fori_loop(LAG, f_tiles, middle, 0)
+    for copy in g_copies:
+        copy.wait()
+    pairs_out[...] = gathered[...]
+    lax.fori_loop(f_tiles - LAG, f_tiles, last, 0)
+
+
+def project(act, perm, wq, wkv, wf):
+    block, depth = act.shape
+    batch = 4 * block
+    f_tiles = wf.shape[1] // TILE
+    width = wq.shape[1] + wkv.shape[1]
+    bf16, f32 = jnp.bfloat16, jnp.float32
+    dma = pltpu.SemaphoreType.DMA
+    vmem = pl.BlockSpec(memory_space=pltpu.VMEM)
+    hbm = pl.BlockSpec(memory_space=pl.ANY)
+    return pl.pallas_call(
+        project_kernel,
+        out_shape=(
+            jax.ShapeDtypeStruct((block, wf.shape[1]), bf16),
+            jax.ShapeDtypeStruct((4, block, width), bf16),
+        ),
+        in_specs=[vmem, vmem, hbm, hbm, hbm],
+        out_specs=(vmem, vmem),
+        scratch_shapes=[
+            pltpu.VMEM((SLOTS, depth, TILE), bf16),
+            pltpu.VMEM((depth, wkv.shape[1]), bf16),
+            pltpu.VMEM((batch, depth), bf16),
+            pltpu.VMEM((batch, depth), bf16),
+            pltpu.VMEM((batch, TILE), f32),
+            pltpu.VMEM((f_tiles, block, TILE), f32),
+            pltpu.VMEM((f_tiles, 3, block, TILE), bf16),
+            pltpu.VMEM((f_tiles, 3, block, TILE), bf16),
+            pltpu.VMEM((block, width), f32),
+            pltpu.VMEM((3, block, width), f32),
+            pltpu.VMEM((3, block, width), f32),
+            pltpu.VMEM((block, width), bf16),
+            pltpu.VMEM((4, block, width), bf16),
+            dma((SLOTS,)),
+            dma(()),
+            dma((3,)),
+            dma((3,)),
+            dma((f_tiles, 3)),
+            dma((f_tiles, 3)),
+            dma((3,)),
+            dma((3,)),
+            dma((3,)),
+            dma((3,)),
+        ],
+        compiler_params=pltpu.CompilerParams(
+            collective_id=0, has_side_effects=True, vmem_limit_bytes=60 * 1024 * 1024
+        ),
+        cost_estimate=pl.CostEstimate(
+            flops=2 * batch * depth * (width + wf.shape[1]),
+            bytes_accessed=2 * depth * (width + wf.shape[1]),
+            transcendentals=block * wf.shape[1],
+        ),
+    )(act, perm, wq, wkv, wf)
+
+
+def fused_shards(
+    activations,
+    query_weight,
+    kv_weight,
+    ffn_weight,
+    cache_keys,
+    cache_values,
+    cache_lengths,
+    slot_rows,
+):
+    slots = slot_rows.shape[0]
+    rows = lax.broadcasted_iota(jnp.int32, (slots, slots), 1)
+    perm = (slot_rows[:, None] == rows).astype(jnp.bfloat16)
+    ffn_hidden, pairs = project(activations, perm, query_weight, kv_weight, ffn_weight)
+    per_device = cache_keys.shape[0]
+    q_width = query_weight.shape[1]
+    mine = lax.dynamic_slice_in_dim(pairs, lax.axis_index("gy") * per_device, per_device, axis=1)
+    mine = mine.transpose(1, 0, 2)
+    query_heads = mine[..., :q_width].reshape(per_device, -1, DH)
+    pair_own = mine[..., q_width:].reshape(per_device, -1)
+    attended = attend(
+        query_heads, pair_own[:, :DH], pair_own[:, DH:], cache_keys, cache_values, cache_lengths
+    )
+    return (attended, ffn_hidden)
+
+
 def solution(mesh):
+    small = mesh.shape["gx"] == 4 and mesh.shape["gy"] == 4
     in_specs = (
         P(("groups", "gy"), "gx"),
         P("gx", "gy"),
@@ -87,4 +330,5 @@
         P("groups"),
     )
     out_specs = (P(("groups", "gx", "gy"), None), P(("groups", "gx"), "gy"))
-    return jax.shard_map(shards, mesh=mesh, in_specs=in_specs, out_specs=out_specs, check_vma=False)
+    body = fused_shards if small else shards
+    return jax.shard_map(body, mesh=mesh, in_specs=in_specs, out_specs=out_specs, check_vma=False)

time: 129 us -> 55.2 us (0.43)
  the two profiles are of different devices: /device:TPU:0 before, /device:TPU:13 now
where the time goes in v1:
time: 55.2 us; the launch traced here: 54.9 us
  Pallas kernels  47.6 us (86%)
  local copies, waits for them, and re-layouts  3.37 us (6%)
  other arithmetic  2.36 us (4%)
  matrix products  0.92 us (2%)
  between operations  0.71 us (1%)
    pallas_call x1, Pallas kernels, project(): pl.pallas_call(project_kernel, out_shape=(jax.ShapeDtypeStruct((block, wf...  47.6 us
    unnamed x6, local copies, waits for them, and re-layouts  2.35 us
    convert_element_type x1, other arithmetic, fused_shards(): perm = (slot_rows[:, None] == rows).astype(jnp.bfloat16)  1.34 us

profile of v1, /device:TPU:13, one launch (start us, length us, event | category | flops | bytes accessed | tf_op | source)
XLA Modules:
  0.0 54.9 jit_solution(5275732220886375572)
XLA Ops:
  0.6 0.0 copy-start
  0.6 0.8 %iota_compare_fusion.1 = pred[4,512]{1,0:T(4,128)(4,1)S(1)} fusion(s32[4]{0:T(128)} %param.14), kind=kLoop, calls=%fused_computation.13 | loop fusion | flops 2048 | bytes 2064 | tf_op jit(solution)/shard_map/lt | solution.py:26
  1.5 1.3 %fusion.6.perm = bf16[64,64]{1,0:T(8,128)(2,1)} fusion(s32[64]{0:T(128)} %param.15), kind=kLoop, calls=%fused_computation.12 | loop fusion | flops 8192 | bytes 8448 | tf_op jit(solution)/shard_map/convert_element_type | solution.py:306
  2.8 0.0 copy-start.1
  2.8 47.6 %shard_map.95 = (bf16[16,9216]{1,0:T(8,128)(2,1)}, bf16[4,16,1664]{2,1,0:T(8,128)(2,1)}) custom-call(bf16[16,4608]{1,0:T(8,128)(2,1)} %act.1, bf16[64,64]{1,0:T(8,128)(2,1)} %fusion.6.perm, bf16[4608,1536]{1,0:T(8,128)(2,1)} %wq.1, bf16[4608,128]{1,0:T(8,128)(2,1)} %wkv.1, bf16[4608,9216]{1,0:T(8,128)(2,1)} %wf.1), custom_call_target="tpu_custom_call" | custom-call | flops 6417285120 | bytes 100270080 | tf_op jit(solution)/shard_map/pallas_call | solution.py:250
  50.4 0.9 %dynamic-slice_bitcast_fusion = bf16[4,4,1664]{2,0,1:T(4,128)(2,1)S(1)} fusion(bf16[4,16,1664]{2,1,0:T(8,128)(2,1)} %get-tuple-element.4, s32[]{:T(128)S(6)} %select_n.7), kind=kLoop, calls=%fused_computation.10 | loop fusion | bytes 106500 | tf_op jit(solution)/shard_map/transpose | solution.py:311
  51.4 0.1 fusion.7
  51.6 0.0 copy-done
  51.6 0.5 fusion.11
  52.1 0.2 fusion.3
  52.3 0.0 copy-done.1
  52.3 0.3 fusion.2
  52.6 0.6 %copy.13 = bf16[1,4,24,256]{3,1,2,0:T(4,128)(2,1)} copy(bf16[1,4,24,256]{3,2,1,0:T(8,128)(2,1)S(1)} %fusion.2) | data formatting | bytes 98304
  53.3 1.7 %copy.17 = bf16[16,9216]{1,0:T(8,128)(2,1)} copy(bf16[16,9216]{1,0:T(8,128)(2,1)} %get-tuple-element.15) | data formatting | bytes 589824
  (7 shorter events, 0.1 us)
Async XLA Ops:
  0.6 50.9 %copy-start = (bf16[4,512,256]{2,1,0:T(8,128)(2,1)S(1)}, bf16[4,512,256]{2,1,0:T(8,128)(2,1)}, u32[]{:S(2)}) copy-start(bf16[4,512,256]{2,1,0:T(8,128)(2,1)} %param.12) | copy-start | bytes 3145732
  2.8 49.5 %copy-start.1 = (bf16[4,512,256]{2,1,0:T(8,128)(2,1)S(1)}, bf16[4,512,256]{2,1,0:T(8,128)(2,1)}, u32[]{:S(2)}) copy-start(bf16[4,512,256]{2,1,0:T(8,128)(2,1)} %param.13) | copy-start | bytes 3145732

commit v2 on v0

--- a/solution.py
+++ b/solution.py
@@ -1,7 +1,14 @@
 import jax
 import jax.numpy as jnp
 from jax import lax
+from jax.experimental import pallas as pl
+from jax.experimental.pallas import tpu as pltpu
 from jax.sharding import PartitionSpec as P
+
+TILE = 512
+SLOTS = 10
+LAG = 3
+CHUNKS = 4
 
 DH = 256
 
@@ -75,7 +82,342 @@
     return (attended, ffn_hidden)
 
 
+def send(src, dst, send_sem, recv_sem, axis, peer):
+    return pltpu.make_async_remote_copy(
+        src_ref=src,
+        dst_ref=dst,
+        send_sem=send_sem,
+        recv_sem=recv_sem,
+        device_id={axis: peer},
+        device_id_type=pl.DeviceIdType.MESH,
+    )
+
+
+def project_kernel(
+    act, slots, lengths, wq, wkv, wf, keys, values,
+    attended_out, hidden_out,
+    wbuf, kvbuf, rows, perm, acc, kv_acc, part, own, fsend, frecv, qown, qsend, qrecv, pair_own,
+    gathered, wide, kbuf, vbuf, flat,
+    c_sem, wsem, kvsem, cache_sem, a_send, a_recv, f_send, f_recv, q_send, q_recv, g_send, g_recv,
+):
+    f32, bf16 = jnp.float32, jnp.bfloat16
+    gx, gy = lax.axis_index("gx"), lax.axis_index("gy")
+    q_width = wq.shape[1]
+    q_tiles = q_width // TILE
+    f_tiles = wf.shape[1] // TILE
+    ahead = SLOTS - q_tiles
+    block, depth = act.shape
+    chunk = depth // CHUNKS
+    kv_width = kvbuf.shape[1]
+
+    def tile_columns(t):
+        return pl.ds(pl.multiple_of(t * TILE, TILE), TILE)
+
+    def load_chunk(c, i):
+        features = pl.ds(c * chunk, chunk)
+        if i < q_tiles:
+            source = wq.at[features, pl.ds(i * TILE, TILE)]
+        else:
+            source = wf.at[features, pl.ds((i - q_tiles) * TILE, TILE)]
+        return pltpu.make_async_copy(source, wbuf.at[i, features], c_sem.at[c, i])
+
+    def await_chunk(c, i):
+        features = pl.ds(c * chunk, chunk)
+        here = wbuf.at[i, features]
+        pltpu.make_async_copy(wf.at[features, pl.ds(0, TILE)], here, c_sem.at[c, i]).wait()
+
+    def load_f(t):
+        slot = lax.rem(t + q_tiles, SLOTS)
+        return pltpu.make_async_copy(wf.at[:, tile_columns(t)], wbuf.at[slot], wsem.at[slot])
+
+    load_kv = pltpu.make_async_copy(wkv, kvbuf, kvsem)
+    load_keys = pltpu.make_async_copy(keys, kbuf, cache_sem.at[0])
+    load_values = pltpu.make_async_copy(values, vbuf, cache_sem.at[1])
+
+    def start_weights(c):
+        for i in range(SLOTS):
+            load_chunk(c, i).start()
+
+    barrier = pltpu.get_barrier_semaphore()
+    for k in range(1, 4):
+        for axis, me in (("gx", gx), ("gy", gy)):
+            pl.semaphore_signal(
+                barrier, inc=1, device_id={axis: lax.rem(me + k, 4)},
+                device_id_type=pl.DeviceIdType.MESH,
+            )
+    start_weights(0)
+    load_kv.start()
+    pl.semaphore_wait(barrier, 6)
+
+    own_rows = pl.ds(pl.multiple_of(gy * block, block), block)
+
+    def row_copy(c, k):
+        features = pl.ds(c * chunk, chunk)
+        return send(
+            act.at[:, features], rows.at[own_rows, features],
+            a_send.at[c, k - 1], a_recv.at[c, k - 1], "gy", lax.rem(gy + k, 4),
+        )
+
+    def start_rows(c):
+        for k in (2, 1, 3):
+            row_copy(c, k).start()
+
+    start_rows(0)
+    start_rows(1)
+    start_weights(1)
+    rows[own_rows, :] = act[...]
+    batch = rows.shape[0]
+    source_row = lax.broadcasted_iota(jnp.int32, (batch, batch), 0)
+    perm[...] = jnp.where(source_row == slots[...], 1.0, 0.0).astype(f32).T.astype(bf16)
+
+    def peer_rows(k):
+        return pl.ds(pl.multiple_of(lax.rem(gx + k, 4) * block, block), block)
+
+    def f_copy(t, k):
+        return send(
+            fsend.at[t, k - 1], frecv.at[t, k - 1], f_send.at[t, k - 1], f_recv.at[t, k - 1],
+            "gx", lax.rem(gx + k, 4),
+        )
+
+    def q_copy(k):
+        return send(
+            qsend.at[k - 1], qrecv.at[k - 1], q_send.at[k - 1], q_recv.at[k - 1],
+            "gx", lax.rem(gx + k, 4),
+        )
+
+    def g_copy(k):
+        return send(
+            pair_own, gathered.at[gy], g_send.at[k - 1], g_recv.at[k - 1],
+            "gy", lax.rem(gy + k, 4),
+        )
+
+    def spread(t):
+        for k in range(1, 4):
+            fsend[t, k - 1] = part[peer_rows(k), :].astype(bf16)
+            f_copy(t, k).start()
+        own[t] = part[peer_rows(0), :]
+
+    def share_queries(width, columns):
+        qown[:, columns] = part[peer_rows(0), :width]
+        for k in range(1, 4):
+            qsend[k - 1, :, columns] = part[peer_rows(k), :width]
+
+    for c in range(CHUNKS):
+        for k in range(1, 4):
+            row_copy(c, k).wait()
+        if c + 2 < CHUNKS:
+            start_rows(c + 2)
+            start_weights(c + 2)
+        features = slice(c * chunk, (c + 1) * chunk)
+        final = c == CHUNKS - 1
+        if c == 0:
+            load_kv.wait()
+        picked = jnp.dot(perm[...], rows[:, features], preferred_element_type=f32).astype(bf16)
+
+        def times(left, right, total, at, c=c):
+            out = jnp.dot(left, right, preferred_element_type=f32)
+            return out if c == 0 else total[at] + out
+
+        for i in range(q_tiles):
+            await_chunk(c, i)
+            out = times(picked, wbuf[i, features, :], acc, i)
+            if final:
+                part[...] = out
+                load_f(jnp.int32(ahead + i)).start()
+                share_queries(TILE, slice(i * TILE, (i + 1) * TILE))
+            else:
+                acc[i] = out
+        out = times(picked, kvbuf[features, :], kv_acc, Ellipsis)
+        if final:
+            part[:, :kv_width] = out
+            share_queries(kv_width, slice(q_width, q_width + kv_width))
+            for k in (2, 1, 3):
+                q_copy(k).start()
+        else:
+            kv_acc[...] = out
+
+        def hidden_chunk(t, carry, c=c, features=features, final=final, times=times):
+            slot = t + q_tiles
+            await_chunk(c, slot)
+            out = times(rows[:, features], wbuf[slot, features, :], acc, slot)
+            if final:
+                part[...] = out
+
+                @pl.when(t + SLOTS < f_tiles)
+                def _():
+                    load_f(t + SLOTS).start()
+
+                spread(t)
+            else:
+                acc[slot] = out
+            return carry
+
+        lax.fori_loop(0, ahead, hidden_chunk, 0)
+
+    def multiply(t):
+        load_f(t).wait()
+        slot = lax.rem(t + q_tiles, SLOTS)
+        part[...] = jnp.dot(rows[...], wbuf[slot], preferred_element_type=f32)
+
+        @pl.when(t + SLOTS < f_tiles)
+        def _():
+            load_f(t + SLOTS).start()
+
+        spread(t)
+
+    def finish(t):
+        total = own[t]
+        for k in range(1, 4):
+            f_copy(t, k).wait()
+            total = total + frecv[t, k - 1].astype(f32)
+        hidden_out[:, tile_columns(t)] = (total / (1.0 + jnp.exp(-total))).astype(bf16)
+
+    def doubled(t, carry):
+        multiply(t)
+        finish(2 * (t - ahead))
+        finish(2 * (t - ahead) + 1)
+        return carry
+
+    def middle(t, carry):
+        multiply(t)
+        finish(t - LAG)
+        return carry
+
+    def last(t, carry):
+        finish(t)
+        return carry
+
+    load_keys.start()
+    load_values.start()
+    even = ahead + ahead - LAG
+    lax.fori_loop(ahead, even, doubled, 0)
+
+    for k in range(1, 4):
+        q_copy(k).wait()
+    pair_own[...] = (qown[...] + qrecv[0] + qrecv[1] + qrecv[2]).astype(bf16)
+    gathered[gy] = pair_own[...]
+    for k in (2, 1, 3):
+        g_copy(k).start()
+
+    lax.fori_loop(even, f_tiles - 2, middle, 0)
+
+    for k in range(1, 4):
+        g_copy(k).wait()
+    wide[...] = gathered[...].astype(f32)
+    load_keys.wait()
+    load_values.wait()
+    count, positions = kbuf.shape[0], kbuf.shape[1]
+    heads = q_width // DH
+    scaling = float(DH) ** (-0.5)
+    for i in range(count):
+        at = pl.ds(gy * count + i, 1)
+        line = [wide[source, at, :] for source in range(4)]
+        query = jnp.concatenate(
+            [line[n][:, h * DH : (h + 1) * DH] for n in range(4) for h in range(heads)], axis=0
+        )
+        pair = jnp.concatenate([line[n][:, q_width:] for n in range(4)], axis=1)
+        new_key, new_value = pair[:, :DH], pair[:, DH:]
+        scores = scaling * lax.dot_general(
+            query.astype(bf16), kbuf[i], (((1,), (1,)), ((), ())), preferred_element_type=f32
+        )
+        new_score = jnp.sum(query * new_key, axis=1, keepdims=True) * scaling
+        usable = lax.broadcasted_iota(jnp.int32, scores.shape, 1) < lengths[i]
+        scores = jnp.where(usable, scores, -jnp.inf)
+        peak = jnp.maximum(jnp.max(scores, axis=1, keepdims=True), new_score)
+        weights = jnp.exp(scores - peak)
+        weight_new = jnp.exp(new_score - peak)
+        totals = jnp.sum(weights, axis=1, keepdims=True) + weight_new
+        probs = (weights / totals).astype(bf16)
+        prob_new = (weight_new / totals).astype(bf16).astype(f32)
+        result = jnp.dot(probs, vbuf[i], preferred_element_type=f32) + prob_new * new_value
+        for h in range(4 * heads):
+            flat[i : i + 1, h * DH : (h + 1) * DH] = result[h : h + 1, :]
+    attended_out[...] = flat[...].astype(bf16)
+
+    lax.fori_loop(f_tiles - 2, f_tiles, middle, 0)
+    lax.fori_loop(f_tiles - LAG, f_tiles, last, 0)
+
+
+def fused_shards(
+    activations,
+    query_weight,
+    kv_weight,
+    ffn_weight,
+    cache_keys,
+    cache_values,
+    cache_lengths,
+    slot_rows,
+):
+    block, depth = activations.shape
+    batch = slot_rows.shape[0]
+    hidden = ffn_weight.shape[1]
+    f_tiles = hidden // TILE
+    kv_width = kv_weight.shape[1]
+    width = query_weight.shape[1] + kv_width
+    count = cache_keys.shape[0]
+    features = 4 * query_weight.shape[1]
+    bf16, f32 = jnp.bfloat16, jnp.float32
+    dma = pltpu.SemaphoreType.DMA
+    vmem = pl.BlockSpec(memory_space=pltpu.VMEM)
+    smem = pl.BlockSpec(memory_space=pltpu.SMEM)
+    hbm = pl.BlockSpec(memory_space=pl.ANY)
+    return pl.pallas_call(
+        project_kernel,
+        out_shape=(
+            jax.ShapeDtypeStruct((count, features), bf16),
+            jax.ShapeDtypeStruct((block, hidden), bf16),
+        ),
+        in_specs=[vmem, vmem, smem, hbm, hbm, hbm, hbm, hbm],
+        out_specs=(vmem, vmem),
+        scratch_shapes=[
+            pltpu.VMEM((SLOTS, depth, TILE), bf16),
+            pltpu.VMEM((depth, kv_width), bf16),
+            pltpu.VMEM((batch, depth), bf16),
+            pltpu.VMEM((batch, batch), bf16),
+            pltpu.VMEM((SLOTS, batch, TILE), f32),
+            pltpu.VMEM((batch, kv_width), f32),
+            pltpu.VMEM((batch, TILE), f32),
+            pltpu.VMEM((f_tiles, block, TILE), f32),
+            pltpu.VMEM((f_tiles, 3, block, TILE), bf16),
+            pltpu.VMEM((f_tiles, 3, block, TILE), bf16),
+            pltpu.VMEM((block, width), f32),
+            pltpu.VMEM((3, block, width), f32),
+            pltpu.VMEM((3, block, width), f32),
+            pltpu.VMEM((block, width), bf16),
+            pltpu.VMEM((4, block, width), bf16),
+            pltpu.VMEM((4, block, width), f32),
+            pltpu.VMEM(cache_keys.shape, bf16),
+            pltpu.VMEM(cache_values.shape, bf16),
+            pltpu.VMEM((count, features), f32),
+            dma((CHUNKS, SLOTS)),
+            dma((SLOTS,)),
+            dma(()),
+            dma((2,)),
+            dma((CHUNKS, 3)),
+            dma((CHUNKS, 3)),
+            dma((f_tiles, 3)),
+            dma((f_tiles, 3)),
+            dma((3,)),
+            dma((3,)),
+            dma((3,)),
+            dma((3,)),
+        ],
+        compiler_params=pltpu.CompilerParams(
+            collective_id=0, has_side_effects=True, vmem_limit_bytes=61 * 1024 * 1024
+        ),
+        cost_estimate=pl.CostEstimate(
+            flops=2 * batch * depth * (width + hidden),
+            bytes_accessed=2 * depth * (width + hidden),
+            transcendentals=block * hidden,
+        ),
+    )(
+        activations, slot_rows.reshape(1, batch), cache_lengths,
+        query_weight, kv_weight, ffn_weight, cache_keys, cache_values,
+    )
+
+
 def solution(mesh):
+    small = mesh.shape["gx"] == 4 and mesh.shape["gy"] == 4
     in_specs = (
         P(("groups", "gy"), "gx"),
         P("gx", "gy"),
@@ -87,4 +429,5 @@
         P("groups"),
     )
     out_specs = (P(("groups", "gx", "gy"), None), P(("groups", "gx"), "gy"))
-    return jax.shard_map(shards, mesh=mesh, in_specs=in_specs, out_specs=out_specs, check_vma=False)
+    body = fused_shards if small else shards
+    return jax.shard_map(body, mesh=mesh, in_specs=in_specs, out_specs=out_specs, check_vma=False)

time: 129 us -> 53.4 us (0.41)
  Pallas kernels: 0 us -> 49.4 us
  matrix products: 42.7 us -> 0 us
  waiting for transfers between devices: 32.7 us -> 0 us
  blocking collectives: 18.4 us -> 0 us
  between operations: 13.8 us -> 0.64 us
  starting transfers between devices: 11.8 us -> 0 us
  other arithmetic: 5.84 us -> 0 us
    pallas_call x0 -> x1, Pallas kernels: none -> 49.4 us  [fused_shards(): pl.pallas_call(project_kernel, out_shape=(jax.ShapeDtypeStruct((count, fe...]
    dot_general x6 -> x0, matrix products: 42.7 us -> none  [the longest x1 31.1 us: shards(): jnp.dot(all_rows, ffn_weight, preferred_element_type=jnp.float32)]
    reduce_scatter x3 -> x0, waiting for transfers between devices: 18.9 us -> none  [the longest x1 18.9 us: shards(): lax.psum_scatter(hidden_part, 'gx', scatter_dimension=1, tiled=True)]
    all_gather x1 -> x0, blocking collectives: 18.4 us -> none  [shards(): all_rows = lax.all_gather(activations, 'gy', axis=0, tiled=True)]
    all_to_all x3 -> x0, waiting for transfers between devices: 13.8 us -> none  [the longest x1 5.65 us: shards(): lax.all_to_all(query_sum.astype(jnp.bfloat16), 'gy', split_axis=0, concat...]
    all_to_all x3 -> x0, starting transfers between devices: 11.7 us -> none  [the longest x1 4.97 us: shards(): lax.all_to_all(pair_sum.astype(jnp.bfloat16), 'gy', split_axis=0, concat_...]
    convert_element_type x5 -> x0, other arithmetic: 4.15 us -> none  [the longest x1 1.94 us: shards(): activated = jax.nn.silu(hidden_sum).astype(jnp.bfloat16)]
    unnamed x7 -> x2, local copies, waits for them, and re-layouts: 0.67 us -> 3.13 us
  transfers between devices with their start and end apart: 6 -> 0, of which waited for: 4 -> 0; matrix products, arithmetic and copies ran while one was open for 35% -> 0% of each run, Pallas kernels for 0% -> 0%
where the time goes in v2:
time: 53.4 us; the launch traced here: 53.1 us
  Pallas kernels  49.4 us (93%)
  local copies, waits for them, and re-layouts  3.13 us (6%)
  between operations  0.64 us (1%)
    pallas_call x1, Pallas kernels, fused_shards(): pl.pallas_call(project_kernel, out_shape=(jax.ShapeDtypeStruct((count, fe...  49.4 us
    unnamed x2, local copies, waits for them, and re-layouts  3.13 us

profile of v2, /device:TPU:0, one launch (start us, length us, event | category | flops | bytes accessed | tf_op | source)
XLA Modules:
  0.0 53.1 jit_solution(14513257777022062800)
XLA Ops:
  0.6 49.4 %shard_map.95 = (bf16[4,6144]{1,0:T(4,128)(2,1)}, bf16[16,9216]{1,0:T(8,128)(2,1)}) custom-call(bf16[16,4608]{1,0:T(8,128)(2,1)} %act.1, s32[1,64]{1,0:T(1,128)} %bitcast.1, s32[4]{0:T(128)} %lengths.1, bf16[4608,1536]{1,0:T(8,128)(2,1)} %wq.1, bf16[4608,128]{1,0:T(8,128)(2,1)} %wkv.1, bf16[4608,9216]{1,0:T(8,128)(2,1)} %wf.1, bf16[4,512,256]{2,1,0:T(8,128)(2,1)} %keys.1, ...), custom_call_target="tpu_custom_call" | custom-call | flops 6417285120 | bytes 100270080 | tf_op jit(solution)/shard_map/pallas_call | solution.py:364
  50.0 1.4 %copy.12 = bf16[4,6144]{1,0:T(4,128)(2,1)} copy(bf16[4,6144]{1,0:T(4,128)(2,1)} %get-tuple-element.4) | data formatting | bytes 98304
  51.4 1.7 %copy.13 = bf16[16,9216]{1,0:T(8,128)(2,1)} copy(bf16[16,9216]{1,0:T(8,128)(2,1)} %get-tuple-element.5) | data formatting | bytes 589824

commit v3 on v2

--- a/solution.py
+++ b/solution.py
@@ -274,13 +274,12 @@
 
     def doubled(t, carry):
         multiply(t)
-        finish(2 * (t - ahead))
-        finish(2 * (t - ahead) + 1)
+        finish(2 * (t - even))
+        finish(2 * (t - even) + 1)
         return carry
 
-    def middle(t, carry):
+    def plain(t, carry):
         multiply(t)
-        finish(t - LAG)
         return carry
 
     def last(t, carry):
@@ -290,7 +289,7 @@
     load_keys.start()
     load_values.start()
     even = ahead + ahead - LAG
-    lax.fori_loop(ahead, even, doubled, 0)
+    lax.fori_loop(ahead, even, plain, 0)
 
     for k in range(1, 4):
         q_copy(k).wait()
@@ -299,7 +298,7 @@
     for k in (2, 1, 3):
         g_copy(k).start()
 
-    lax.fori_loop(even, f_tiles - 2, middle, 0)
+    lax.fori_loop(even, f_tiles - 2, doubled, 0)
 
     for k in range(1, 4):
         g_copy(k).wait()
@@ -334,8 +333,8 @@
             flat[i : i + 1, h * DH : (h + 1) * DH] = result[h : h + 1, :]
     attended_out[...] = flat[...].astype(bf16)
 
-    lax.fori_loop(f_tiles - 2, f_tiles, middle, 0)
-    lax.fori_loop(f_tiles - LAG, f_tiles, last, 0)
+    lax.fori_loop(f_tiles - 2, f_tiles, doubled, 0)
+    lax.fori_loop(2 * (f_tiles - even), f_tiles, last, 0)
 
 
 def fused_shards(

time: 53.4 us -> 50.9 us (0.953)
  Pallas kernels: 49.4 us -> 46.9 us
    pallas_call x1, Pallas kernels: 49.4 us -> 46.9 us  [fused_shards(): pl.pallas_call(project_kernel, out_shape=(jax.ShapeDtypeStruct((count, fe...]
where the time goes in v3:
time: 50.9 us; the launch traced here: 50.7 us
  Pallas kernels  46.9 us (92%)
  local copies, waits for them, and re-layouts  3.13 us (6%)
  between operations  0.64 us (1%)
    pallas_call x1, Pallas kernels, fused_shards(): pl.pallas_call(project_kernel, out_shape=(jax.ShapeDtypeStruct((count, fe...  46.9 us
    unnamed x2, local copies, waits for them, and re-layouts  3.13 us

profile of v3, /device:TPU:0, one launch (start us, length us, event | category | flops | bytes accessed | tf_op | source)
XLA Modules:
  0.0 50.7 jit_solution(9290635425777836785)
XLA Ops:
  0.6 46.9 %shard_map.95 = (bf16[4,6144]{1,0:T(4,128)(2,1)}, bf16[16,9216]{1,0:T(8,128)(2,1)}) custom-call(bf16[16,4608]{1,0:T(8,128)(2,1)} %act.1, s32[1,64]{1,0:T(1,128)} %bitcast.1, s32[4]{0:T(128)} %lengths.1, bf16[4608,1536]{1,0:T(8,128)(2,1)} %wq.1, bf16[4608,128]{1,0:T(8,128)(2,1)} %wkv.1, bf16[4608,9216]{1,0:T(8,128)(2,1)} %wf.1, bf16[4,512,256]{2,1,0:T(8,128)(2,1)} %keys.1, ...), custom_call_target="tpu_custom_call" | custom-call | flops 6417285120 | bytes 100270080 | tf_op jit(solution)/shard_map/pallas_call | solution.py:363
  47.5 1.4 %copy.12 = bf16[4,6144]{1,0:T(4,128)(2,1)} copy(bf16[4,6144]{1,0:T(4,128)(2,1)} %get-tuple-element.4) | data formatting | bytes 98304
  49.0 1.7 %copy.13 = bf16[16,9216]{1,0:T(8,128)(2,1)} copy(bf16[16,9216]{1,0:T(8,128)(2,1)} %get-tuple-element.5) | data formatting | bytes 589824
